TPU v7x, 128 devices: a whole 4x4x4 slice. The times are simulated.
128 devices in a mesh: row: 16 (over z, x_lo, core), col: 8 (over x_hi, y).
Axes of the slice: x: 4 (x_hi: 2, x_lo: 2; x = x_hi * 2 + x_lo), y: 4, z: 4, core: 2. Of those that a mesh axis runs over, the one named last changes fastest.
Arguments:
- tile_values: bfloat16 [32768, 128, 128], P(('row', 'col')), may hold values from -0.09375 to 0.09375
- slot_codes: int32 [32768], P(('row', 'col')), may hold values from -1 to 511, as said below
- right_start: float32 [32768, 256], P(('row', 'col')), may hold values from -6 to 6
- left_start: float32 [32768, 256], P(('row', 'col')), may hold values from -6 to 6
- node_diagonal: float32 [32768], P(('row', 'col')), may hold values from 1 to 3
- row_scale: float32 [32768], P(('row', 'col')), may hold values from 0.2 to 15
Outputs:
- right_block: float32 [32768, 256], P(('row', 'col'))
- left_block: float32 [32768, 256], P(('row', 'col'))
- projections: float32 [2, 256, 256], replicated
Inputs may be any that keep to these rules, and one draw needn't show every extreme that they name: `slot_codes`: slot (s, p, c) carries a tile that device s extracted for owner p; its code is -1 (empty) or a position a 32 + b in p's block grid of 16 x 2 * 16 places. The codes of one owner's live slots over all sources are distinct, so an owner receives at most 128 live tiles, and some owner receives exactly 128. A source fills at most 2 slots for one owner, and some source fills all 2.
All inputs are finite; a program needn't handle non-finite values.
Results may differ from a plain program's by a relative error of at most 0.002.
Values may be sent and summed in bfloat16 or wider, within the bound.
A program may use at most 128 MiB of HBM per device.

v0:
```python
import jax
import jax.numpy as jnp
from jax import lax
from jax.sharding import PartitionSpec as P

ITERS = 2
epsilon = 1e-06


def slot_product(slot_tiles, pick_keys, sum_keys, blocks, key_count, transposed):
    tile_rows = slot_tiles.shape[1]
    port_count = blocks.shape[2]
    slot_total = slot_tiles.shape[0]
    groups = 4
    grouped_tiles = slot_tiles.reshape(groups, slot_total // groups, tile_rows, tile_rows)
    grouped_pick = pick_keys.reshape(groups, slot_total // groups)
    grouped_sum = sum_keys.reshape(groups, slot_total // groups)
    form = "syx,syp->sxp" if transposed else "sxy,syp->sxp"

    def accumulate(summed, group):
        group_tiles, group_pick, group_sum = group
        picked = blocks[group_pick]
        contrib = jnp.einsum(form, group_tiles, picked, preferred_element_type=jnp.float32)
        onehot = (group_sum[:, None] == jnp.arange(key_count)[None, :]).astype(jnp.float32)
        added = jnp.einsum("sn,sxp->nxp", onehot, contrib, precision=lax.Precision.HIGHEST)
        return (summed + added, None)

    start = jnp.zeros((key_count, tile_rows, port_count), jnp.float32)
    summed, _ = lax.scan(accumulate, start, (grouped_tiles, grouped_pick, grouped_sum))
    return summed.reshape(key_count * tile_rows, port_count)


def local(tile_values, slot_codes, right_start, left_start, node_diagonal, row_scale):
    row_size = lax.axis_size("row")
    col_size = lax.axis_size("col")
    owners = row_size * col_size
    tile_rows = tile_values.shape[1]
    port_count = right_start.shape[1]
    order_rows = right_start.shape[0] * owners
    grid_rows = 2 * col_size
    grid_cols = 2 * row_size
    got_tiles, got_codes = (
        lax.all_to_all(tile_values, ("row", "col"), split_axis=0, concat_axis=0, tiled=True),
        lax.all_to_all(slot_codes, ("row", "col"), split_axis=0, concat_axis=0, tiled=True),
    )
    live = got_codes >= 0
    block_row = got_codes // grid_cols
    block_col = got_codes % grid_cols
    row_sum_key = jnp.where(live, block_row, grid_rows)
    col_pick_key = jnp.where(live, block_col, 0)
    row_pick_key = jnp.where(live, block_row, 0)
    col_sum_key = jnp.where(live, block_col, grid_cols)
    scale_col = row_scale[:, None]
    diag_col = node_diagonal[:, None]
    right_vec = right_start
    left_vec = right_start + left_start
    stored = []
    for turn in range(ITERS):
        right_bf = right_vec.astype(jnp.bfloat16)
        scaled_left = scale_col * left_vec
        left_bf = scaled_left.astype(jnp.bfloat16)
        right_cols = lax.all_gather(right_bf, "row", axis=0, tiled=True)
        left_rows = lax.all_gather(left_bf, "col", axis=0, tiled=True)
        right_blocks = right_cols.reshape(grid_cols, tile_rows, port_count)
        right_part = slot_product(
            got_tiles, col_pick_key, row_sum_key, right_blocks, grid_rows, False
        )
        blocks = left_rows.reshape(grid_rows, tile_rows, port_count)
        left_part = slot_product(got_tiles, row_pick_key, col_sum_key, blocks, grid_cols, True)
        right_prod = lax.psum_scatter(right_part, "col", scatter_dimension=0, tiled=True)
        left_prod = lax.psum_scatter(left_part, "row", scatter_dimension=0, tiled=True)
        right_new = scale_col * (right_prod + diag_col * right_vec)
        left_new = left_prod + diag_col * scaled_left
        local_proj = jnp.dot(left_vec.T, right_new, precision=lax.Precision.HIGHEST)
        project = lax.psum(local_proj, ("row", "col")) / order_rows
        right_rest = right_new - jnp.dot(right_vec, project, precision=lax.Precision.HIGHEST)
        left_rest = left_new - jnp.dot(left_vec, project.T, precision=lax.Precision.HIGHEST)
        right_sq, left_sq = lax.psum(
            (jnp.sum(right_rest * right_rest, axis=0), jnp.sum(left_rest * left_rest, axis=0)),
            ("row", "col"),
        )
        right_vec = right_rest / jnp.sqrt(right_sq / order_rows + epsilon)[None, :]
        left_vec = left_rest / jnp.sqrt(left_sq / order_rows + epsilon)[None, :]
        stored.append(project)
    return (right_vec, left_vec, jnp.stack(stored))


def solution(mesh):
    return jax.shard_map(
        local,
        mesh=mesh,
        in_specs=(
            P(("row", "col"), None, None),
            P(("row", "col")),
            P(("row", "col"), None),
            P(("row", "col"), None),
            P(("row", "col")),
            P(("row", "col")),
        ),
        out_specs=(P(("row", "col"), None), P(("row", "col"), None), P()),
        check_vma=False,
    )
```

profile of v0, /device:TPU:1, one launch (start us, length us, event | category | flops | bytes accessed | tf_op | source)
XLA Modules:
  0.0 1186.2 jit_solution(6084935444073180689)
XLA Ops:
  8.0 21.1 %all_to_all.17 = s32[128,2,1]{1,2,0:T(1,128)S(1)} all-to-all(s32[128,2,1]{1,2,0:T(1,128)S(1)} %bitcast.149), channel_id=1, replica_groups=mesh['row'=16,'col'=8] {'row','col'}, dimensions={0} | all-to-all | bytes 2048 | tf_op jit(solution)/shard_map/all_to_all | solution.py:44
  36.8 112.9 %all-gather.5.cloned.1.call-done = bf16[4096,256]{1,0:T(8,128)(2,1)} async-done(((bf16[256,256]{1,0:T(8,128)(2,1)}), bf16[4096,256]{1,0:T(8,128)(2,1)}) %all-gather.5.cloned.1.call-update) | async-done | bytes 2097168 | tf_op jit(solution)/shard_map/all_gather | solution.py:62
  149.7 90.1 %while.44 = (s32[]{:T(128)}, f32[16,128,256]{2,0,1:T(8,128)S(1)}, s32[4,64]{1,0:T(4,128)S(1)}, bf16[4,64,128,128]{3,2,1,0:T(8,128)(2,1)}, s32[4,64]{1,0:T(4,128)...) while((s32[]{:T(128)}, f32[16,128,256]{2,0,1:T(8,128)S(1)}, ...), condition=%wide.region_1.2_spmd.clone, body=%wide.region_0.1_spmd.clone.sunk | while | flops 940574912 | bytes 35658084 | solution.py:29
  154.1 7.3 fusion.117
  161.3 10.8 select_add_fusion.8
  176.6 7.3 fusion.117
  183.9 10.8 select_add_fusion.8
  199.1 7.3 fusion.117
  206.4 10.8 select_add_fusion.8
  221.6 7.3 fusion.117
  228.9 10.8 select_add_fusion.8
  243.1 12.0 %copy.22 = bf16[256,128,128]{1,2,0:T(8,128)(2,1)} copy(bf16[256,128,128]{2,1,0:T(8,128)(2,1)} %all-to-all-done.1) | data formatting | bytes 16777216 | tf_op jit(solution)/shard_map/all_to_all | solution.py:43
  255.1 61.6 %reduce-scatter.5.cloned.1.call-done = f32[256,256]{1,0:T(8,128)} async-done(((f32[2048,256]{1,0:T(8,128)}), f32[256,256]{1,0:T(8,128)}) %reduce-scatter.5.cloned.1.call-update) | async-done | bytes 262160 | tf_op jit(solution)/shard_map/reduce_scatter | solution.py:70
  319.7 45.1 %all-gather.9.cloned.1.call-done = bf16[2048,256]{1,0:T(8,128)(2,1)} async-done(((bf16[256,256]{1,0:T(8,128)(2,1)}), bf16[2048,256]{1,0:T(8,128)(2,1)}) %all-gather.9.cloned.1.call-update) | async-done | bytes 1048592 | tf_op jit(solution)/shard_map/all_gather | solution.py:63
  364.8 101.9 %while.46 = (s32[]{:T(128)}, f32[32,128,256]{2,0,1:T(8,128)}, s32[4,64]{1,0:T(4,128)S(1)}, bf16[4,64,128,128]{2,3,1,0:T(8,128)(2,1)}, s32[4,64]{1,0:T(4,128)S(1)...) while((s32[]{:T(128)}, f32[32,128,256]{2,0,1:T(8,128)}, s32[4,64]{1,0:T(4,128)S(1)}, ...), condition=%wide.region_10.11_spmd.clone, body=%wide.region_9.10_spmd.clone.sunk | while | flops 1344277760 | bytes 39852388 | solution.py:29
  368.8 7.3 fusion.131
  376.1 13.3 %select_add_fusion.10 = f32[32,128,256]{2,0,1:T(8,128)} fusion(f32[32,128,256]{2,0,1:T(8,128)} %get-tuple-element.481, f32[64,128,256]{2,1,0:T(8,128)} %fusion.131, pred[]{:T(512)S(6)} %compare.21, s32[64]{0:T(128)S(1)} %fusion.132), kind=kOutput, calls=%fused_computation.40.clone.1 | convolution fusion | flops 807405568 | bytes 16777472 | tf_op jit(solution)/shard_map/while/body/eval_jaxpr/sn,sxp->nxp/dot_general | solution.py:25
  393.4 7.3 fusion.131
  400.7 14.4 %select_add_fusion.10 = f32[32,128,256]{2,0,1:T(8,128)} fusion(f32[32,128,256]{2,0,1:T(8,128)} %get-tuple-element.481, f32[64,128,256]{2,1,0:T(8,128)} %fusion.131, pred[]{:T(512)S(6)} %compare.21, s32[64]{0:T(128)S(1)} %fusion.132), kind=kOutput, calls=%fused_computation.40.clone.1 | convolution fusion | flops 807405568 | bytes 16777472 | tf_op jit(solution)/shard_map/while/body/eval_jaxpr/sn,sxp->nxp/dot_general | solution.py:25
  419.1 7.3 fusion.131
  426.4 14.4 %select_add_fusion.10 = f32[32,128,256]{2,0,1:T(8,128)} fusion(f32[32,128,256]{2,0,1:T(8,128)} %get-tuple-element.481, f32[64,128,256]{2,1,0:T(8,128)} %fusion.131, pred[]{:T(512)S(6)} %compare.21, s32[64]{0:T(128)S(1)} %fusion.132), kind=kOutput, calls=%fused_computation.40.clone.1 | convolution fusion | flops 807405568 | bytes 16777472 | tf_op jit(solution)/shard_map/while/body/eval_jaxpr/sn,sxp->nxp/dot_general | solution.py:25
  444.8 7.3 fusion.131
  452.1 14.4 %select_add_fusion.10 = f32[32,128,256]{2,0,1:T(8,128)} fusion(f32[32,128,256]{2,0,1:T(8,128)} %get-tuple-element.481, f32[64,128,256]{2,1,0:T(8,128)} %fusion.131, pred[]{:T(512)S(6)} %compare.21, s32[64]{0:T(128)S(1)} %fusion.132), kind=kOutput, calls=%fused_computation.40.clone.1 | convolution fusion | flops 807405568 | bytes 16777472 | tf_op jit(solution)/shard_map/while/body/eval_jaxpr/sn,sxp->nxp/dot_general | solution.py:25
  473.4 38.5 %all-reduce.5.cloned.1.call-done = f32[256,256]{1,0:T(8,128)} async-done(((f32[256,256]{1,0:T(8,128)}), f32[256,256]{1,0:T(8,128)}) %all-reduce.5.cloned.1.call-update) | async-done | bytes 262160 | tf_op jit(solution)/shard_map/psum | solution.py:75
  513.2 66.1 %reduce-scatter.9.cloned.1.call-done = f32[256,256]{1,0:T(8,128)} async-done(((f32[4096,256]{1,0:T(8,128)}), f32[256,256]{1,0:T(8,128)}) %reduce-scatter.9.cloned.1.call-update) | async-done | bytes 262160 | tf_op jit(solution)/shard_map/reduce_scatter | solution.py:71
  580.8 67.3 %all-reduce.1 = (f32[256]{0:T(256)S(1)}, f32[256]{0:T(256)S(1)}) all-reduce(f32[256]{0:T(256)S(1)} %get-tuple-element.290, f32[256]{0:T(256)S(1)} %get-tuple-element.292), channel_id=1, replica_groups=mesh['row'=16,'col'=8] {'row','col'}, use_global_device_ids=true, to_apply=%region_5.6 | all-reduce | flops 512 | bytes 4096 | tf_op jit(solution)/shard_map/psum | solution.py:78
  648.8 31.3 %all-gather.7.cloned.1.call-done = bf16[4096,256]{1,0:T(8,128)(2,1)} async-done(((bf16[256,256]{1,0:T(8,128)(2,1)}), bf16[4096,256]{1,0:T(8,128)(2,1)}) %all-gather.7.cloned.1.call-update) | async-done | bytes 2097168 | tf_op jit(solution)/shard_map/all_gather | solution.py:62
  680.1 90.2 %while.45 = (s32[]{:T(128)}, f32[16,128,256]{2,0,1:T(8,128)S(1)}, s32[4,64]{1,0:T(4,128)S(1)}, bf16[4,64,128,128]{3,2,1,0:T(8,128)(2,1)}, s32[4,64]{1,0:T(4,128)...) while((s32[]{:T(128)}, f32[16,128,256]{2,0,1:T(8,128)S(1)}, ...), condition=%wide.region_7.8_spmd.clone, body=%wide.region_6.7_spmd.clone.sunk | while | flops 940574912 | bytes 35658084 | solution.py:29
  691.8 10.8 select_add_fusion.9
  707.1 7.3 fusion.124
  714.4 10.8 select_add_fusion.9
  736.9 10.8 select_add_fusion.9
  752.2 7.3 fusion.124
  759.5 10.8 select_add_fusion.9
  773.9 72.2 %reduce-scatter.7.cloned.1.call-done = f32[256,256]{1,0:T(8,128)} async-done(((f32[2048,256]{1,0:T(8,128)}), f32[256,256]{1,0:T(8,128)}) %reduce-scatter.7.cloned.1.call-update) | async-done | bytes 262160 | tf_op jit(solution)/shard_map/reduce_scatter | solution.py:70
  848.5 45.6 %all-gather.11.cloned.1.call-done = bf16[2048,256]{1,0:T(8,128)(2,1)} async-done(((bf16[256,256]{1,0:T(8,128)(2,1)}), bf16[2048,256]{1,0:T(8,128)(2,1)}) %all-gather.11.cloned.1.call-update) | async-done | bytes 1048592 | tf_op jit(solution)/shard_map/all_gather | solution.py:63
  894.1 102.2 %while.47 = (s32[]{:T(128)}, f32[32,128,256]{2,0,1:T(8,128)}, s32[4,64]{1,0:T(4,128)S(1)}, bf16[4,64,128,128]{2,3,1,0:T(8,128)(2,1)}, s32[4,64]{1,0:T(4,128)S(1)...) while((s32[]{:T(128)}, f32[32,128,256]{2,0,1:T(8,128)}, s32[4,64]{1,0:T(4,128)S(1)}, ...), condition=%wide.region_18.19_spmd.clone, body=%wide.region_17.18_spmd.clone.sunk | while | flops 1344277760 | bytes 39852388 | solution.py:29
  898.3 7.3 fusion.138
  905.6 13.2 %select_add_fusion.11 = f32[32,128,256]{2,0,1:T(8,128)} fusion(f32[32,128,256]{2,0,1:T(8,128)} %get-tuple-element.529, f32[64,128,256]{2,1,0:T(8,128)} %fusion.138, pred[]{:T(512)S(6)} %compare.22, s32[64]{0:T(128)S(1)} %fusion.139), kind=kOutput, calls=%fused_computation.57.clone.1 | convolution fusion | flops 807405568 | bytes 16777472 | tf_op jit(solution)/shard_map/while/body/eval_jaxpr/sn,sxp->nxp/dot_general | solution.py:25
  922.9 7.3 fusion.138
  930.2 14.4 %select_add_fusion.11 = f32[32,128,256]{2,0,1:T(8,128)} fusion(f32[32,128,256]{2,0,1:T(8,128)} %get-tuple-element.529, f32[64,128,256]{2,1,0:T(8,128)} %fusion.138, pred[]{:T(512)S(6)} %compare.22, s32[64]{0:T(128)S(1)} %fusion.139), kind=kOutput, calls=%fused_computation.57.clone.1 | convolution fusion | flops 807405568 | bytes 16777472 | tf_op jit(solution)/shard_map/while/body/eval_jaxpr/sn,sxp->nxp/dot_general | solution.py:25
  948.7 7.3 fusion.138
  956.0 14.4 %select_add_fusion.11 = f32[32,128,256]{2,0,1:T(8,128)} fusion(f32[32,128,256]{2,0,1:T(8,128)} %get-tuple-element.529, f32[64,128,256]{2,1,0:T(8,128)} %fusion.138, pred[]{:T(512)S(6)} %compare.22, s32[64]{0:T(128)S(1)} %fusion.139), kind=kOutput, calls=%fused_computation.57.clone.1 | convolution fusion | flops 807405568 | bytes 16777472 | tf_op jit(solution)/shard_map/while/body/eval_jaxpr/sn,sxp->nxp/dot_general | solution.py:25
  974.4 7.3 fusion.138
  981.7 14.4 %select_add_fusion.11 = f32[32,128,256]{2,0,1:T(8,128)} fusion(f32[32,128,256]{2,0,1:T(8,128)} %get-tuple-element.529, f32[64,128,256]{2,1,0:T(8,128)} %fusion.138, pred[]{:T(512)S(6)} %compare.22, s32[64]{0:T(128)S(1)} %fusion.139), kind=kOutput, calls=%fused_computation.57.clone.1 | convolution fusion | flops 807405568 | bytes 16777472 | tf_op jit(solution)/shard_map/while/body/eval_jaxpr/sn,sxp->nxp/dot_general | solution.py:25
  1003.9 37.4 %all-reduce.7.cloned.1.call-done = f32[256,256]{1,0:T(8,128)} async-done(((f32[256,256]{1,0:T(8,128)}), f32[256,256]{1,0:T(8,128)}) %all-reduce.7.cloned.1.call-update) | async-done | bytes 262160 | tf_op jit(solution)/shard_map/psum | solution.py:75
  1044.5 64.3 %reduce-scatter.11.cloned.1.call-done = f32[256,256]{1,0:T(8,128)} async-done(((f32[4096,256]{1,0:T(8,128)}), f32[256,256]{1,0:T(8,128)}) %reduce-scatter.11.cloned.1.call-update) | async-done | bytes 262160 | tf_op jit(solution)/shard_map/reduce_scatter | solution.py:71
  1110.2 67.3 %all-reduce = (f32[256]{0:T(256)S(1)}, f32[256]{0:T(256)S(1)}) all-reduce(f32[256]{0:T(256)S(1)} %get-tuple-element.294, f32[256]{0:T(256)S(1)} %get-tuple-element.296), channel_id=1, replica_groups=mesh['row'=16,'col'=8] {'row','col'}, use_global_device_ids=true, to_apply=%region_16.17 | all-reduce | flops 512 | bytes 4096 | tf_op jit(solution)/shard_map/psum | solution.py:78
  (132 shorter events, 126.1 us)
Async XLA Ops:
  29.1 5.4 copy-start.1
  29.1 5.4 copy-start.3
  29.1 5.4 copy-start.4
  29.1 120.6 %all-to-all-start.1 = ((bf16[256,128,128]{2,1,0:T(8,128)(2,1)}), bf16[256,128,128]{2,1,0:T(8,128)(2,1)}, u32[]{:S(2)}, u32[]{:S(2)}) async-start(bf16[256,128,128]{2,1,0:T(8,128)(2,1)} %param.14), calls=%async_computation.1 | async-start | bytes 16777216 | tf_op jit(solution)/shard_map/all_to_all | solution.py:43
  34.4 115.3 %all-gather.5.cloned.1.call-start = ((), (), s32[]{:S(2)}) async-start(), calls=%async_computation.6 | async-start | bytes 2228224 | tf_op jit(solution)/shard_map/all_gather | solution.py:62
  35.3 281.5 %reduce-scatter.5.cloned.1.call-start = ((), (), s32[]{:S(2)}) async-start(), calls=%async_computation.7 | async-start | bytes 2359296 | tf_op jit(solution)/shard_map/reduce_scatter | solution.py:70
  242.3 122.5 %all-gather.9.cloned.1.call-start = ((), (), s32[]{:S(2)}) async-start(), calls=%async_computation.11 | async-start | bytes 1179648 | tf_op jit(solution)/shard_map/all_gather | solution.py:63
  243.1 268.8 %all-reduce.5.cloned.1.call-start = ((), (), s32[]{:S(2)}) async-start(), calls=%async_computation.8 | async-start | bytes 524288 | tf_op jit(solution)/shard_map/psum | solution.py:75
  243.1 73.6 %copy-start.5 = (f32[256]{0:T(256)S(1)}, f32[256]{0:T(256)}, u32[]{:S(2)}) copy-start(f32[256]{0:T(256)} %param.18) | copy-start | bytes 3076
  319.1 260.2 %reduce-scatter.9.cloned.1.call-start = ((), (), s32[]{:S(2)}) async-start(), calls=%async_computation.12 | async-start | bytes 4456448 | tf_op jit(solution)/shard_map/reduce_scatter | solution.py:71
  473.3 38.6 %copy-start.2 = (f32[256,256]{1,0:T(8,128)S(1)}, f32[256,256]{1,0:T(8,128)}, u32[]{:S(2)}) copy-start(f32[256,256]{1,0:T(8,128)} %reduce-scatter.5.cloned.1.call-done) | copy-start | bytes 786436
  473.3 206.8 %all-gather.7.cloned.1.call-start = ((), (), s32[]{:S(2)}) async-start(), calls=%async_computation.9 | async-start | bytes 2228224 | tf_op jit(solution)/shard_map/all_gather | solution.py:62
  648.8 197.3 %reduce-scatter.7.cloned.1.call-start = ((), (), s32[]{:S(2)}) async-start(), calls=%async_computation.10 | async-start | bytes 2359296 | tf_op jit(solution)/shard_map/reduce_scatter | solution.py:70
  773.0 121.1 %all-gather.11.cloned.1.call-start = ((), (), s32[]{:S(2)}) async-start(), calls=%async_computation.14 | async-start | bytes 1179648 | tf_op jit(solution)/shard_map/all_gather | solution.py:63
  773.8 267.5 %all-reduce.7.cloned.1.call-start = ((), (), s32[]{:S(2)}) async-start(), calls=%async_computation.13 | async-start | bytes 524288 | tf_op jit(solution)/shard_map/psum | solution.py:75
  848.4 260.3 %reduce-scatter.11.cloned.1.call-start = ((), (), s32[]{:S(2)}) async-start(), calls=%async_computation.15 | async-start | bytes 4456448 | tf_op jit(solution)/shard_map/reduce_scatter | solution.py:71
  1002.9 0.9 copy-start
  1002.9 40.2 %copy-start.6 = (f32[256,256]{1,0:T(8,128)S(1)}, f32[256,256]{1,0:T(8,128)}, u32[]{:S(2)}) copy-start(f32[256,256]{1,0:T(8,128)} %reduce-scatter.7.cloned.1.call-done) | copy-start | bytes 786436
Sparse Core Ops, SparseCore 0:
  37.5 112.1 all-gather.4
  242.5 74.2 reduce-scatter.4
  319.7 45.0 all-gather.8
  370.0 141.8 all-reduce.4
  514.1 65.1 reduce-scatter.8
  648.9 31.1 all-gather.6
  773.1 72.9 reduce-scatter.6
  849.0 45.0 all-gather.10
  899.4 141.8 all-reduce.6
  1043.5 65.1 reduce-scatter.10
where the time goes:
time: 1200 us; the launch traced here: 1190 us
  waiting for transfers between devices  576 us (48%)
  matrix products  327 us (27%)
  blocking collectives  156 us (13%)
  local copies, waits for them, and re-layouts  99.6 us (8%)
  between operations  14.8 us (1%)
    dot_general x16, matrix products, accumulate(): jnp.einsum('sn,sxp->nxp', onehot, contrib, precision=lax.Precision.HIGHEST)  200 us
    all_gather x2, waiting for transfers between devices, local(): right_cols = lax.all_gather(right_bf, 'row', axis=0, tiled=True)  144 us
    psum x2, blocking collectives, local(): lax.psum((jnp.sum(right_rest * right_rest, axis=0), jnp.sum(left_rest * l...  135 us
    reduce_scatter x2, waiting for transfers between devices, local(): lax.psum_scatter(right_part, 'col', scatter_dimension=0, tiled=True)  134 us
    reduce_scatter x2, waiting for transfers between devices, local(): lax.psum_scatter(left_part, 'row', scatter_dimension=0, tiled=True)  130 us
    dot_general x16, matrix products, accumulate(): jnp.einsum(form, group_tiles, picked, preferred_element_type=jnp.float32)  117 us
    all_gather x2, waiting for transfers between devices, local(): left_rows = lax.all_gather(left_bf, 'col', axis=0, tiled=True)  90.7 us
    psum x2, waiting for transfers between devices, local(): project = lax.psum(local_proj, ('row', 'col')) / order_rows  75.9 us
  transfers between devices with their start and end apart: 11, of which 10 were waited for; matrix products, arithmetic and copies ran while one was open for 20% of the time, Pallas kernels for 0%

commit v1 on v0

--- a/solution.py
+++ b/solution.py
@@ -60,7 +60,9 @@
         scaled_left = scale_col * left_vec
         left_bf = scaled_left.astype(jnp.bfloat16)
         right_cols = lax.all_gather(right_bf, "row", axis=0, tiled=True)
-        left_rows = lax.all_gather(left_bf, "col", axis=0, tiled=True)
+        left_rows = jnp.concatenate(
+            lax.all_to_all(jnp.stack([left_bf] * lax.axis_size("col")), "col", 0, 0), axis=0
+        )
         right_blocks = right_cols.reshape(grid_cols, tile_rows, port_count)
         right_part = slot_product(
             got_tiles, col_pick_key, row_sum_key, right_blocks, grid_rows, False

time: 1200 us -> 1110 us (0.925)
  waiting for transfers between devices: 576 us -> 486 us
  starting transfers between devices: 6.25 us -> 19.6 us
    all_gather x2 -> x0, waiting for transfers between devices: 90.7 us -> none  [local(): left_rows = lax.all_gather(left_bf, 'col', axis=0, tiled=True)]
    all_to_all x0 -> x2, starting transfers between devices: none -> 13.5 us  [local(): lax.all_to_all(jnp.stack([left_bf] * lax.axis_size('col')), 'col', 0, 0)]
  transfers between devices with their start and end apart: 11 -> 11, of which waited for: 10 -> 8; matrix products, arithmetic and copies ran while one was open for 20% -> 21% of each run, Pallas kernels for 0% -> 0%
where the time goes in v1:
time: 1110 us; the launch traced here: 1100 us
  waiting for transfers between devices  486 us (44%)
  matrix products  327 us (29%)
  blocking collectives  156 us (14%)
  local copies, waits for them, and re-layouts  91.8 us (8%)
  starting transfers between devices  19.6 us (2%)
  between operations  14.8 us (1%)
    dot_general x16, matrix products, accumulate(): jnp.einsum('sn,sxp->nxp', onehot, contrib, precision=lax.Precision.HIGHEST)  200 us
    all_gather x2, waiting for transfers between devices, local(): right_cols = lax.all_gather(right_bf, 'row', axis=0, tiled=True)  144 us
    psum x2, blocking collectives, local(): lax.psum((jnp.sum(right_rest * right_rest, axis=0), jnp.sum(left_rest * l...  135 us
    reduce_scatter x2, waiting for transfers between devices, local(): lax.psum_scatter(right_part, 'col', scatter_dimension=0, tiled=True)  131 us
    reduce_scatter x2, waiting for transfers between devices, local(): lax.psum_scatter(left_part, 'row', scatter_dimension=0, tiled=True)  130 us
    dot_general x16, matrix products, accumulate(): jnp.einsum(form, group_tiles, picked, preferred_element_type=jnp.float32)  117 us
    psum x2, waiting for transfers between devices, local(): project = lax.psum(local_proj, ('row', 'col')) / order_rows  80.5 us
    gather x16, local copies, waits for them, and re-layouts, accumulate(): picked = blocks[group_pick]  57 us
  transfers between devices with their start and end apart: 11, of which 8 were waited for; matrix products, arithmetic and copies ran while one was open for 21% of the time, Pallas kernels for 0%

profile of v1, /device:TPU:1, one launch (start us, length us, event | category | flops | bytes accessed | tf_op | source)
XLA Modules:
  0.0 1101.5 jit_solution(11841523673451084229)
XLA Ops:
  8.0 21.1 %all_to_all.27 = s32[128,2,1]{1,2,0:T(1,128)S(1)} all-to-all(s32[128,2,1]{1,2,0:T(1,128)S(1)} %bitcast.149), channel_id=1, replica_groups=mesh['row'=16,'col'=8] {'row','col'}, dimensions={0} | all-to-all | bytes 2048 | tf_op jit(solution)/shard_map/all_to_all | solution.py:44
  36.7 112.9 %all-gather.3.cloned.1.call-done = bf16[4096,256]{1,0:T(8,128)(2,1)} async-done(((bf16[256,256]{1,0:T(8,128)(2,1)}), bf16[4096,256]{1,0:T(8,128)(2,1)}) %all-gather.3.cloned.1.call-update) | async-done | bytes 2097168 | tf_op jit(solution)/shard_map/all_gather | solution.py:62
  149.7 90.1 %while.44 = (s32[]{:T(128)}, f32[16,128,256]{2,0,1:T(8,128)S(1)}, s32[4,64]{1,0:T(4,128)S(1)}, bf16[4,64,128,128]{3,2,1,0:T(8,128)(2,1)}, s32[4,64]{1,0:T(4,128)...) while((s32[]{:T(128)}, f32[16,128,256]{2,0,1:T(8,128)S(1)}, ...), condition=%wide.region_1.2_spmd.clone, body=%wide.region_0.1_spmd.clone.sunk | while | flops 940574912 | bytes 35658084 | solution.py:29
  154.1 7.3 fusion.117
  161.3 10.8 select_add_fusion.8
  176.6 7.3 fusion.117
  183.9 10.8 select_add_fusion.8
  199.1 7.3 fusion.117
  206.4 10.8 select_add_fusion.8
  221.6 7.3 fusion.117
  228.9 10.8 select_add_fusion.8
  243.4 7.4 all-to-all-start.2
  250.9 12.0 %copy.22 = bf16[256,128,128]{1,2,0:T(8,128)(2,1)} copy(bf16[256,128,128]{2,1,0:T(8,128)(2,1)} %all-to-all-done.1) | data formatting | bytes 16777216 | tf_op jit(solution)/shard_map/all_to_all | solution.py:43
  262.9 59.4 %reduce-scatter.5.cloned.1.call-done = f32[256,256]{1,0:T(8,128)} async-done(((f32[2048,256]{1,0:T(8,128)}), f32[256,256]{1,0:T(8,128)}) %reduce-scatter.5.cloned.1.call-update) | async-done | bytes 262160 | tf_op jit(solution)/shard_map/reduce_scatter | solution.py:72
  325.3 96.9 %while.46 = (s32[]{:T(128)}, f32[32,128,256]{2,0,1:T(8,128)}, s32[4,64]{1,0:T(4,128)S(1)}, bf16[4,64,128,128]{2,3,1,0:T(8,128)(2,1)}, s32[4,64]{1,0:T(4,128)S(1)...) while((s32[]{:T(128)}, f32[32,128,256]{2,0,1:T(8,128)}, s32[4,64]{1,0:T(4,128)S(1)}, ...), condition=%wide.region_10.11_spmd.clone, body=%wide.region_9.10_spmd.clone.sunk | while | flops 1344277760 | bytes 39852388 | solution.py:29
  335.3 13.3 %select_add_fusion.10 = f32[32,128,256]{2,0,1:T(8,128)} fusion(f32[32,128,256]{2,0,1:T(8,128)} %get-tuple-element.481, f32[64,128,256]{2,1,0:T(8,128)} %fusion.131, pred[]{:T(512)S(6)} %compare.21, s32[64]{0:T(128)S(1)} %fusion.132), kind=kOutput, calls=%fused_computation.40.clone.1 | convolution fusion | flops 807405568 | bytes 16777472 | tf_op jit(solution)/shard_map/while/body/eval_jaxpr/sn,sxp->nxp/dot_general | solution.py:25
  351.3 7.3 fusion.131
  358.7 14.4 %select_add_fusion.10 = f32[32,128,256]{2,0,1:T(8,128)} fusion(f32[32,128,256]{2,0,1:T(8,128)} %get-tuple-element.481, f32[64,128,256]{2,1,0:T(8,128)} %fusion.131, pred[]{:T(512)S(6)} %compare.21, s32[64]{0:T(128)S(1)} %fusion.132), kind=kOutput, calls=%fused_computation.40.clone.1 | convolution fusion | flops 807405568 | bytes 16777472 | tf_op jit(solution)/shard_map/while/body/eval_jaxpr/sn,sxp->nxp/dot_general | solution.py:25
  375.8 7.3 fusion.131
  383.1 14.4 %select_add_fusion.10 = f32[32,128,256]{2,0,1:T(8,128)} fusion(f32[32,128,256]{2,0,1:T(8,128)} %get-tuple-element.481, f32[64,128,256]{2,1,0:T(8,128)} %fusion.131, pred[]{:T(512)S(6)} %compare.21, s32[64]{0:T(128)S(1)} %fusion.132), kind=kOutput, calls=%fused_computation.40.clone.1 | convolution fusion | flops 807405568 | bytes 16777472 | tf_op jit(solution)/shard_map/while/body/eval_jaxpr/sn,sxp->nxp/dot_general | solution.py:25
  400.3 7.3 fusion.131
  407.6 14.4 %select_add_fusion.10 = f32[32,128,256]{2,0,1:T(8,128)} fusion(f32[32,128,256]{2,0,1:T(8,128)} %get-tuple-element.481, f32[64,128,256]{2,1,0:T(8,128)} %fusion.131, pred[]{:T(512)S(6)} %compare.21, s32[64]{0:T(128)S(1)} %fusion.132), kind=kOutput, calls=%fused_computation.40.clone.1 | convolution fusion | flops 807405568 | bytes 16777472 | tf_op jit(solution)/shard_map/while/body/eval_jaxpr/sn,sxp->nxp/dot_general | solution.py:25
  428.8 40.6 %all-reduce.5.cloned.1.call-done = f32[256,256]{1,0:T(8,128)} async-done(((f32[256,256]{1,0:T(8,128)}), f32[256,256]{1,0:T(8,128)}) %all-reduce.5.cloned.1.call-update) | async-done | bytes 262160 | tf_op jit(solution)/shard_map/psum | solution.py:77
  470.9 66.0 %reduce-scatter.9.cloned.1.call-done = f32[256,256]{1,0:T(8,128)} async-done(((f32[4096,256]{1,0:T(8,128)}), f32[256,256]{1,0:T(8,128)}) %reduce-scatter.9.cloned.1.call-update) | async-done | bytes 262160 | tf_op jit(solution)/shard_map/reduce_scatter | solution.py:73
  538.3 67.4 %all-reduce.1 = (f32[256]{0:T(256)S(1)}, f32[256]{0:T(256)S(1)}) all-reduce(f32[256]{0:T(256)S(1)} %get-tuple-element.290, f32[256]{0:T(256)S(1)} %get-tuple-element.292), channel_id=1, replica_groups=mesh['row'=16,'col'=8] {'row','col'}, use_global_device_ids=true, to_apply=%region_5.6 | all-reduce | flops 512 | bytes 4096 | tf_op jit(solution)/shard_map/psum | solution.py:80
  606.5 31.2 %all-gather.5.cloned.1.call-done = bf16[4096,256]{1,0:T(8,128)(2,1)} async-done(((bf16[256,256]{1,0:T(8,128)(2,1)}), bf16[4096,256]{1,0:T(8,128)(2,1)}) %all-gather.5.cloned.1.call-update) | async-done | bytes 2097168 | tf_op jit(solution)/shard_map/all_gather | solution.py:62
  637.7 90.1 %while.45 = (s32[]{:T(128)}, f32[16,128,256]{2,0,1:T(8,128)S(1)}, s32[4,64]{1,0:T(4,128)S(1)}, bf16[4,64,128,128]{3,2,1,0:T(8,128)(2,1)}, s32[4,64]{1,0:T(4,128)...) while((s32[]{:T(128)}, f32[16,128,256]{2,0,1:T(8,128)S(1)}, ...), condition=%wide.region_7.8_spmd.clone, body=%wide.region_6.7_spmd.clone.sunk | while | flops 940574912 | bytes 35658084 | solution.py:29
  642.0 7.3 fusion.124
  649.3 10.8 select_add_fusion.9
  664.6 7.3 fusion.124
  671.9 10.8 select_add_fusion.9
  687.1 7.3 fusion.124
  694.4 10.8 select_add_fusion.9
  709.7 7.3 fusion.124
  716.9 10.8 select_add_fusion.9
  737.7 71.4 %reduce-scatter.7.cloned.1.call-done = f32[256,256]{1,0:T(8,128)} async-done(((f32[2048,256]{1,0:T(8,128)}), f32[256,256]{1,0:T(8,128)}) %reduce-scatter.7.cloned.1.call-update) | async-done | bytes 262160 | tf_op jit(solution)/shard_map/reduce_scatter | solution.py:72
  811.6 97.4 %while.47 = (s32[]{:T(128)}, f32[32,128,256]{2,0,1:T(8,128)}, s32[4,64]{1,0:T(4,128)S(1)}, bf16[4,64,128,128]{2,3,1,0:T(8,128)(2,1)}, s32[4,64]{1,0:T(4,128)S(1)...) while((s32[]{:T(128)}, f32[32,128,256]{2,0,1:T(8,128)}, ...), condition=%wide.region_18.19_spmd.clone, body=%wide.region_17.18_spmd.clone.sunk | while | flops 1344277760 | bytes 39852388 | solution.py:29
  814.6 7.3 fusion.138
  821.9 13.3 %select_add_fusion.11 = f32[32,128,256]{2,0,1:T(8,128)} fusion(f32[32,128,256]{2,0,1:T(8,128)} %get-tuple-element.529, f32[64,128,256]{2,1,0:T(8,128)} %fusion.138, pred[]{:T(512)S(6)} %compare.22, s32[64]{0:T(128)S(1)} %fusion.139), kind=kOutput, calls=%fused_computation.57.clone.1 | convolution fusion | flops 807405568 | bytes 16777472 | tf_op jit(solution)/shard_map/while/body/eval_jaxpr/sn,sxp->nxp/dot_general | solution.py:25
  838.0 7.3 fusion.138
  845.3 14.4 %select_add_fusion.11 = f32[32,128,256]{2,0,1:T(8,128)} fusion(f32[32,128,256]{2,0,1:T(8,128)} %get-tuple-element.529, f32[64,128,256]{2,1,0:T(8,128)} %fusion.138, pred[]{:T(512)S(6)} %compare.22, s32[64]{0:T(128)S(1)} %fusion.139), kind=kOutput, calls=%fused_computation.57.clone.1 | convolution fusion | flops 807405568 | bytes 16777472 | tf_op jit(solution)/shard_map/while/body/eval_jaxpr/sn,sxp->nxp/dot_general | solution.py:25
  862.5 7.3 fusion.138
  869.8 14.4 %select_add_fusion.11 = f32[32,128,256]{2,0,1:T(8,128)} fusion(f32[32,128,256]{2,0,1:T(8,128)} %get-tuple-element.529, f32[64,128,256]{2,1,0:T(8,128)} %fusion.138, pred[]{:T(512)S(6)} %compare.22, s32[64]{0:T(128)S(1)} %fusion.139), kind=kOutput, calls=%fused_computation.57.clone.1 | convolution fusion | flops 807405568 | bytes 16777472 | tf_op jit(solution)/shard_map/while/body/eval_jaxpr/sn,sxp->nxp/dot_general | solution.py:25
  887.0 7.3 fusion.138
  894.4 14.4 %select_add_fusion.11 = f32[32,128,256]{2,0,1:T(8,128)} fusion(f32[32,128,256]{2,0,1:T(8,128)} %get-tuple-element.529, f32[64,128,256]{2,1,0:T(8,128)} %fusion.138, pred[]{:T(512)S(6)} %compare.22, s32[64]{0:T(128)S(1)} %fusion.139), kind=kOutput, calls=%fused_computation.57.clone.1 | convolution fusion | flops 807405568 | bytes 16777472 | tf_op jit(solution)/shard_map/while/body/eval_jaxpr/sn,sxp->nxp/dot_general | solution.py:25
  916.6 39.8 %all-reduce.7.cloned.1.call-done = f32[256,256]{1,0:T(8,128)} async-done(((f32[256,256]{1,0:T(8,128)}), f32[256,256]{1,0:T(8,128)}) %all-reduce.7.cloned.1.call-update) | async-done | bytes 262160 | tf_op jit(solution)/shard_map/psum | solution.py:77
  959.5 64.5 %reduce-scatter.11.cloned.1.call-done = f32[256,256]{1,0:T(8,128)} async-done(((f32[4096,256]{1,0:T(8,128)}), f32[256,256]{1,0:T(8,128)}) %reduce-scatter.11.cloned.1.call-update) | async-done | bytes 262160 | tf_op jit(solution)/shard_map/reduce_scatter | solution.py:73
  1025.5 67.3 %all-reduce = (f32[256]{0:T(256)S(1)}, f32[256]{0:T(256)S(1)}) all-reduce(f32[256]{0:T(256)S(1)} %get-tuple-element.294, f32[256]{0:T(256)S(1)} %get-tuple-element.296), channel_id=1, replica_groups=mesh['row'=16,'col'=8] {'row','col'}, use_global_device_ids=true, to_apply=%region_16.17 | all-reduce | flops 512 | bytes 4096 | tf_op jit(solution)/shard_map/psum | solution.py:80
  (132 shorter events, 115.6 us)
Async XLA Ops:
  29.1 5.4 copy-start.1
  29.1 5.4 copy-start.3
  29.1 5.4 copy-start.4
  29.1 120.6 %all-to-all-start.1 = ((bf16[256,128,128]{2,1,0:T(8,128)(2,1)}), bf16[256,128,128]{2,1,0:T(8,128)(2,1)}, u32[]{:S(2)}, u32[]{:S(2)}) async-start(bf16[256,128,128]{2,1,0:T(8,128)(2,1)} %param.14), calls=%async_computation.1 | async-start | bytes 16777216 | tf_op jit(solution)/shard_map/all_to_all | solution.py:43
  34.4 115.3 %all-gather.3.cloned.1.call-start = ((), (), s32[]{:S(2)}) async-start(), calls=%async_computation.8 | async-start | bytes 2228224 | tf_op jit(solution)/shard_map/all_gather | solution.py:62
  35.2 287.1 %reduce-scatter.5.cloned.1.call-start = ((), (), s32[]{:S(2)}) async-start(), calls=%async_computation.9 | async-start | bytes 2359296 | tf_op jit(solution)/shard_map/reduce_scatter | solution.py:72
  243.4 81.8 %all-to-all-start.2 = ((bf16[8,256,256]{2,1,0:T(8,128)(2,1)}), bf16[8,256,256]{2,1,0:T(8,128)(2,1)S(1)}, u32[]{:S(2)}, u32[]{:S(2)}) async-start(bf16[8,256,256]{2,1,0:T(8,128)(2,1)} %stack.10), calls=%async_computation.4 | async-start | bytes 2097152 | tf_op jit(solution)/shard_map/all_to_all | solution.py:64
  250.8 218.7 %all-reduce.5.cloned.1.call-start = ((), (), s32[]{:S(2)}) async-start(), calls=%async_computation.10 | async-start | bytes 524288 | tf_op jit(solution)/shard_map/psum | solution.py:77
  250.9 71.4 %copy-start.5 = (f32[256]{0:T(256)S(1)}, f32[256]{0:T(256)}, u32[]{:S(2)}) copy-start(f32[256]{0:T(256)} %param.18) | copy-start | bytes 3076
  324.7 212.2 %reduce-scatter.9.cloned.1.call-start = ((), (), s32[]{:S(2)}) async-start(), calls=%async_computation.13 | async-start | bytes 4456448 | tf_op jit(solution)/shard_map/reduce_scatter | solution.py:73
  428.8 40.7 %copy-start.2 = (f32[256,256]{1,0:T(8,128)S(1)}, f32[256,256]{1,0:T(8,128)}, u32[]{:S(2)}) copy-start(f32[256,256]{1,0:T(8,128)} %reduce-scatter.5.cloned.1.call-done) | copy-start | bytes 786436
  428.8 208.9 %all-gather.5.cloned.1.call-start = ((), (), s32[]{:S(2)}) async-start(), calls=%async_computation.11 | async-start | bytes 2228224 | tf_op jit(solution)/shard_map/all_gather | solution.py:62
  606.4 202.7 %reduce-scatter.7.cloned.1.call-start = ((), (), s32[]{:S(2)}) async-start(), calls=%async_computation.12 | async-start | bytes 2359296 | tf_op jit(solution)/shard_map/reduce_scatter | solution.py:72
  731.6 80.0 %all-to-all-start.3 = ((bf16[8,256,256]{2,1,0:T(8,128)(2,1)}), bf16[8,256,256]{2,1,0:T(8,128)(2,1)S(1)}, u32[]{:S(2)}, u32[]{:S(2)}) async-start(bf16[8,256,256]{2,1,0:T(8,128)(2,1)} %stack.11), calls=%async_computation.6 | async-start | bytes 2097152 | tf_op jit(solution)/shard_map/all_to_all | solution.py:64
  737.7 218.7 %all-reduce.7.cloned.1.call-start = ((), (), s32[]{:S(2)}) async-start(), calls=%async_computation.14 | async-start | bytes 524288 | tf_op jit(solution)/shard_map/psum | solution.py:77
  811.5 212.5 %reduce-scatter.11.cloned.1.call-start = ((), (), s32[]{:S(2)}) async-start(), calls=%async_computation.15 | async-start | bytes 4456448 | tf_op jit(solution)/shard_map/reduce_scatter | solution.py:73
  915.6 0.9 copy-start
  915.6 42.6 %copy-start.6 = (f32[256,256]{1,0:T(8,128)S(1)}, f32[256,256]{1,0:T(8,128)}, u32[]{:S(2)}) copy-start(f32[256,256]{1,0:T(8,128)} %reduce-scatter.7.cloned.1.call-done) | copy-start | bytes 786436
Sparse Core Ops, SparseCore 0:
  37.5 112.1 all-gather.2
  242.5 79.7 reduce-scatter.4
  327.6 141.8 all-reduce.4
  471.7 65.0 reduce-scatter.8
  606.5 31.0 all-gather.4
  730.5 78.5 reduce-scatter.6
  814.5 141.8 all-reduce.6
  958.8 65.1 reduce-scatter.10
